TPU v7x, 256 devices: a whole 4x4x8 slice. The times are simulated.
256 devices in a mesh: row: 32 (over x, y, core), col: 8 (over z).
Axes of the slice: x: 4, y: 4, z: 8, core: 2. Of those that a mesh axis runs over, the one named last changes fastest.
Arguments:
- psi: bfloat16 [81920, 64], P('row'), may hold values from -6 to 6
- block_len: int32 [320], P('row'), may hold values from 1 to 256, as said below
- targets: int32 [320, 4], P('row'), may hold values from 0 to 319, as said below
- counts: int32 [320], P('row'), may hold values from 1 to 4, as said below
- dipole: bfloat16 [320, 4, 256, 256], P('row', None, 'col'), may hold values from -0.25 to 0.25
- eigvec: bfloat16 [81920, 8192], P('row', 'col'), may hold values from -0.03125 to 0.03125
Outputs:
- elements: float32 [8192, 64], P('col')
Inputs may be any that keep to these rules, and one draw needn't show every extreme that they name: `block_len`: some block has length 256 and some length 1. `targets`: each target lies within 2 blocks of its own block; some lie exactly 2 below and 2 above. `counts`: some block uses all 4 slots.
All inputs are finite; a program needn't handle non-finite values.
Results may differ from a plain program's by a relative error of at most 0.003.
Values may be sent and summed in bfloat16 or wider, within the bound.
A program may use at most 64 MiB of HBM per device.

v0:
```python
import jax
import jax.numpy as jnp
from jax import lax
from jax.sharding import PartitionSpec as P

WB = 2


def extended_2(cells, sides, width):
    for axis, dim in sides:
        count = lax.axis_size(axis)
        ends = count - 1
        head = lax.slice_in_dim(cells, 0, width, axis=dim)
        tail = lax.slice_in_dim(cells, cells.shape[dim] - width, cells.shape[dim], axis=dim)
        cells = jnp.concatenate(
            [
                lax.ppermute(tail, axis, [(i, (i + 1) % count) for i in range(ends)]),
                cells,
                lax.ppermute(head, axis, [((i + 1) % count, i) for i in range(ends)]),
            ],
            axis=dim,
        )
    return cells


def on_device(psi, block_len, targets, counts, dipole, eigvec):
    owned_blocks = block_len.shape[0]
    slot_total = dipole.shape[1]
    col_rows = dipole.shape[2]
    block_rows = dipole.shape[3]
    state_count = psi.shape[1]
    row_count = lax.axis_size("row")
    sub_rows = col_rows // row_count
    positions = jnp.arange(block_rows, dtype=jnp.int32)
    row_used = positions[None, :] < block_len[:, None]
    blocks = psi.reshape(owned_blocks, block_rows, state_count)
    blocks = jnp.where(row_used[:, :, None], blocks, jnp.zeros((), jnp.bfloat16))
    extended = extended_2(blocks, (("row", 0),), WB)
    offset_start = lax.axis_index("row") * owned_blocks - WB
    chosen = extended[targets - offset_start]
    slot_index = jnp.arange(slot_total, dtype=jnp.int32)
    slot_flags = slot_index[None, :] < counts[:, None]
    chosen = jnp.where(slot_flags[:, :, None, None], chosen, jnp.zeros((), jnp.bfloat16))
    product = jnp.einsum("bkrs,bksn->brn", dipole, chosen, preferred_element_type=jnp.float32)
    global_rows = lax.axis_index("col") * col_rows + jnp.arange(col_rows, dtype=jnp.int32)
    rows_kept = global_rows[None, :] < block_len[:, None]
    product = jnp.where(rows_kept[:, :, None], product, jnp.float32(0.0)).astype(jnp.bfloat16)
    pieces = product.reshape(1, owned_blocks, row_count, sub_rows, state_count)
    gathered = lax.all_gather(pieces, "col", axis=0, tiled=True)
    arranged = lax.all_to_all(gathered, "row", split_axis=2, concat_axis=1, tiled=True)
    flat_rows = arranged.reshape(-1, state_count)
    partial_sum = lax.dot_general(
        eigvec, flat_rows, (((0,), (0,)), ((), ())), preferred_element_type=jnp.float32
    )
    return lax.psum(partial_sum, "row")


def solution(mesh):
    placed = (
        P("row", None),
        P("row"),
        P("row", None),
        P("row"),
        P("row", None, "col", None),
        P("row", "col"),
    )
    return jax.shard_map(
        on_device, mesh=mesh, in_specs=placed, out_specs=P("col", None), check_vma=False
    )
```

profile of v0, /device:TPU:1, one launch (start us, length us, event | category | flops | bytes accessed | tf_op | source)
XLA Modules:
  0.0 186.5 jit_solution(11062037817866423832)
XLA Ops:
  6.5 0.0 copy-start
  6.5 0.0 all-reduce.2.cloned.1.call-start
  6.5 0.8 iota_compare_fusion
  7.3 1.0 bitcast_select_fusion
  8.4 4.6 %collective-permute-start = (bf16[2,256,64]{1,2,0:T(8,128)(2,1)S(1)}, bf16[2,256,64]{1,2,0:T(8,128)(2,1)S(1)}, u32[]{:S(2)}, u32[]{:S(2)}) collective-permute-start(bf16[2,256,64]{1,2,0:T(8,128)(2,1)S(1)} %get-tuple-element.5), channel_id=1, source_target_pairs={{0,8},{8,16},{16,24},{24,32},{32,40},{40,48},{48,56},{56,64},{64,7... | collective-permute-start | bytes 196616 | tf_op jit(solution)/shard_map/ppermute | solution.py:17
  13.0 1.9 %collective-permute-start.1 = (bf16[2,256,64]{1,2,0:T(8,128)(2,1)S(1)}, bf16[2,256,64]{1,2,0:T(8,128)(2,1)S(1)}, u32[]{:S(2)}, u32[]{:S(2)}) collective-permute-start(bf16[2,256,64]{1,2,0:T(8,128)(2,1)S(1)} %get-tuple-element.6), channel_id=1, source_target_pairs={{8,0},{16,8},{24,16},{32,24},{40,32},{48,40},{56,48},{64,56},{72,6... | collective-permute-start | bytes 196616 | tf_op jit(solution)/shard_map/ppermute | solution.py:19
  14.9 0.7 compare_select_fusion
  15.6 0.1 copy.13
  15.7 0.1 reshape.87
  15.8 0.7 broadcast_compare_fusion
  16.5 0.7 iota_compare_fusion.1
  17.2 0.0 collective-permute-done
  17.3 1.3 collective-permute-done.1
  18.5 0.1 pad_maximum_fusion
  18.6 0.6 gather_fusion
  19.3 0.0 copy-done
  19.3 0.5 fusion.12
  19.8 24.1 %all-gather = bf16[80,32,64]{2,1,0:T(8,128)(2,1)S(1)} all-gather(bf16[10,32,64]{2,1,0:T(8,128)(2,1)S(1)} %fusion.12), channel_id=2, replica_groups=mesh['row'=32,'col'=8] {'col'}, dimensions={0}, use_global_device_ids=true | all-gather | bytes 368640 | tf_op jit(solution)/shard_map/all_gather | solution.py:49
  43.9 0.4 copy.20
  44.3 0.4 reshape.97
  44.7 21.4 %all_to_all.15 = bf16[32,2,2560]{2,1,0:T(2,128)(2,1)S(1)} all-to-all(bf16[32,2,2560]{2,1,0:T(2,128)(2,1)S(1)} %reshape.97), channel_id=1, replica_groups=mesh['row'=32,'col'=8] {'row'}, dimensions={0} | all-to-all | bytes 655360 | tf_op jit(solution)/shard_map/all_to_all | solution.py:50
  66.1 0.4 reshape.98
  66.6 0.2 copy.15
  66.8 0.4 reshape.84
  67.1 4.2 %convolution_bitcast_fusion = f32[1024,64]{0,1:T(8,128)} fusion(bf16[2560,64]{1,0:T(8,128)(2,1)S(1)} %reshape.84, bf16[2560,1024]{1,0:T(8,128)(2,1)} %param.11), kind=kOutput, calls=%fused_computation.4 | convolution fusion | flops 335544320 | bytes 5832704 | tf_op jit(solution)/shard_map/dot_general | solution.py:52
  71.4 0.0 all-reduce.2.cloned.1.call-update
  71.4 106.5 %all-reduce.2.cloned.1.call-done = f32[1024,64]{0,1:T(8,128)} async-done(((f32[1024,64]{0,1:T(8,128)}), f32[1024,64]{0,1:T(8,128)}) %all-reduce.2.cloned.1.call-update) | async-done | bytes 262160 | tf_op jit(solution)/shard_map/psum | solution.py:55
  177.9 1.7 copy.22
  (4 shorter events, 0.1 us)
Async XLA Ops:
  6.5 12.7 %copy-start = (bf16[10,4,32,256]{3,2,1,0:T(8,128)(2,1)S(1)}, bf16[10,4,32,256]{3,2,1,0:T(8,128)(2,1)}, u32[]{:S(2)}) copy-start(bf16[10,4,32,256]{3,2,1,0:T(8,128)(2,1)} %param.10) | copy-start | bytes 1966084
  6.5 171.4 %all-reduce.2.cloned.1.call-start = ((), (), s32[]{:S(2)}) async-start(), calls=%async_computation.1 | async-start | bytes 524288 | tf_op jit(solution)/shard_map/psum | solution.py:55
  8.4 8.9 %collective-permute-start = (bf16[2,256,64]{1,2,0:T(8,128)(2,1)S(1)}, bf16[2,256,64]{1,2,0:T(8,128)(2,1)S(1)}, u32[]{:S(2)}, u32[]{:S(2)}) collective-permute-start(bf16[2,256,64]{1,2,0:T(8,128)(2,1)S(1)} %get-tuple-element.5), channel_id=1, source_target_pairs={{0,8},{8,16},{16,24},{24,32},{32,40},{40,48},{48,56},{56,64},{64,7... | collective-permute-start | bytes 196616 | tf_op jit(solution)/shard_map/ppermute | solution.py:17
  13.0 5.6 %collective-permute-start.1 = (bf16[2,256,64]{1,2,0:T(8,128)(2,1)S(1)}, bf16[2,256,64]{1,2,0:T(8,128)(2,1)S(1)}, u32[]{:S(2)}, u32[]{:S(2)}) collective-permute-start(bf16[2,256,64]{1,2,0:T(8,128)(2,1)S(1)} %get-tuple-element.6), channel_id=1, source_target_pairs={{8,0},{16,8},{24,16},{32,24},{40,32},{48,40},{56,48},{64,56},{72,6... | collective-permute-start | bytes 196616 | tf_op jit(solution)/shard_map/ppermute | solution.py:19
Sparse Core Ops, SparseCore 0:
  71.5 106.3 all-reduce.1
where the time goes:
time: 187 us; the launch traced here: 186 us
  waiting for transfers between devices  108 us (58%)
  blocking collectives  45.5 us (24%)
  between operations  13.5 us (7%)
  starting transfers between devices  6.52 us (3%)
  matrix products  4.79 us (3%)
  local copies, waits for them, and re-layouts  4.32 us (2%)
  other arithmetic  4.01 us (2%)
    psum x1, waiting for transfers between devices, on_device(): return lax.psum(partial_sum, 'row')  107 us
    all_gather x1, blocking collectives, on_device(): gathered = lax.all_gather(pieces, 'col', axis=0, tiled=True)  24.1 us
    all_to_all x1, blocking collectives, on_device(): lax.all_to_all(gathered, 'row', split_axis=2, concat_axis=1, tiled=True)  21.4 us
    ppermute x1, starting transfers between devices, extended_2(): lax.ppermute(tail, axis, [(i, (i + 1) % count) for i in range(ends)])  4.59 us
    dot_general x1, matrix products, on_device(): lax.dot_general(eigvec, flat_rows, (((0,), (0,)), ((), ())), preferred_el...  4.24 us
  transfers between devices with their start and end apart: 3, of which 2 were waited for; matrix products, arithmetic and copies ran while one was open for 1% of the time, Pallas kernels for 0%

commit v1 on v0

v1 whole, which is shorter than its diff:
```python
import functools

import jax
import jax.numpy as jnp
from jax import lax
from jax.experimental import pallas as pl
from jax.experimental.pallas import tpu as pltpu
from jax.sharding import PartitionSpec as P

WB = 2
MESH = pl.DeviceIdType.MESH
NT = (((1,), (1,)), ((), ()))
PAD = 16


def body(
    n_row, n_col, nb, kmax, bs, st,
    lens, targets, counts, psi_hbm, dip_hbm, eig_hbm, out_ref,
    psi_v, ext, dip_v, eig_v, stage, msg, recv, gath, acc, rs_recv,
    ld_sem, halo_send, halo_recv, a2a_send, a2a_recv, z_send, z_recv,
    rs_send, rs_sem, ag_send, ag_sem,
):
    row = lax.axis_index("row")
    col = lax.axis_index("col")
    piece = nb * n_row
    f32, bf16 = jnp.float32, jnp.bfloat16

    ld_psi = pltpu.make_async_copy(psi_hbm, psi_v, ld_sem.at[0])
    ld_dip = pltpu.make_async_copy(dip_hbm, dip_v, ld_sem.at[1])
    ld_eig = pltpu.make_async_copy(eig_hbm, eig_v, ld_sem.at[2])
    ld_psi.start()
    ld_dip.start()
    ld_eig.start()

    barrier = pltpu.get_barrier_semaphore()

    def greet_row(i, carry):
        pl.semaphore_signal(
            barrier, inc=1, device_id=(lax.rem(row + i, n_row), col), device_id_type=MESH
        )
        return carry

    def greet_col(i, carry):
        pl.semaphore_signal(
            barrier, inc=1, device_id=(row, lax.rem(col + i, n_col)), device_id_type=MESH
        )
        return carry

    lax.fori_loop(1, n_row, greet_row, 0)
    lax.fori_loop(1, n_col, greet_col, 0)

    stage[...] = jnp.zeros_like(stage)
    ld_psi.wait()
    lane = lax.broadcasted_iota(jnp.int32, (st, bs), 1)
    order = list(range(WB)) + list(range(nb - WB, nb)) + list(range(WB, nb - WB))
    for b in order:
        block = psi_v[:, b * bs : (b + 1) * bs]
        ext[b + WB] = jnp.where(lane < lens[b], block, jnp.zeros((), bf16))

    wanted = lax.broadcasted_iota(jnp.int32, (n_row * PAD, piece), 1)
    wanted = wanted + (PAD - nb) * (wanted // nb)
    have = lax.broadcasted_iota(jnp.int32, (n_row * PAD, piece), 0)
    select = jnp.where(have == wanted, 1.0, 0.0).astype(bf16)

    pl.semaphore_wait(barrier, n_row - 1 + n_col - 1)

    right = lax.rem(row + 1, n_row)
    left = lax.rem(row + n_row - 1, n_row)
    to_right = pltpu.make_async_remote_copy(
        src_ref=ext.at[pl.ds(nb, WB)], dst_ref=ext.at[pl.ds(0, WB)],
        send_sem=halo_send.at[0], recv_sem=halo_recv.at[0],
        device_id=(right, col), device_id_type=MESH,
    )
    to_left = pltpu.make_async_remote_copy(
        src_ref=ext.at[pl.ds(WB, WB)], dst_ref=ext.at[pl.ds(nb + WB, WB)],
        send_sem=halo_send.at[1], recv_sem=halo_recv.at[1],
        device_id=(left, col), device_id_type=MESH,
    )
    to_right.start()
    to_left.start()
    ld_dip.wait()
    to_right.wait()
    to_left.wait()

    first = row * nb - WB
    sub = n_row
    kept = lax.broadcasted_iota(jnp.int32, (sub, st), 0) + col * sub
    for b in range(nb):
        total = jnp.zeros((sub, st), f32)
        for k in range(kmax):
            chosen = ext[jnp.clip(targets[k, b] - first, b, b + 2 * WB)]
            chosen = jnp.where(k < counts[b], chosen, jnp.zeros((), bf16))
            total += lax.dot_general(dip_v[b, k], chosen, NT, preferred_element_type=f32)
        total = jnp.where(kept < lens[b], total, 0.0)
        stage[pl.ds(b, sub, stride=PAD), :] = total
    msg[...] = stage[...].astype(bf16).reshape(msg.shape)

    def send_piece(i, carry):
        to = lax.rem(row + i, n_row)
        pltpu.make_async_remote_copy(
            src_ref=msg.at[to], dst_ref=recv.at[row],
            send_sem=a2a_send, recv_sem=a2a_recv,
            device_id=(to, col), device_id_type=MESH,
        ).start()
        return carry

    lax.fori_loop(1, n_row, send_piece, 0)
    recv[row] = msg[row]
    many = pl.ds(0, n_row - 1)
    pltpu.make_async_copy(recv.at[many], recv.at[many], a2a_recv).wait()

    rows = recv[...].reshape(n_row * PAD, st)
    turned = lax.dot_general(
        rows, select, (((0,), (0,)), ((), ())), preferred_element_type=f32
    ).astype(bf16)
    half = st // 2
    gath[col, 0:st, :] = turned[:, 0:128]
    gath[col, st : 2 * st, :] = turned[:, 128:256]
    gath[col, 2 * st : 2 * st + half, :] = jnp.concatenate(
        [turned[:half, 256:320], turned[half:, 256:320]], axis=1
    )

    hops = [(s + 1) // 2 if s % 2 else n_col - s // 2 for s in range(1, n_col)]
    for d in hops:
        pltpu.make_async_remote_copy(
            src_ref=gath.at[col], dst_ref=gath.at[col],
            send_sem=z_send, recv_sem=z_recv.at[col],
            device_id=(row, lax.rem(col + d, n_col)), device_id_type=MESH,
        ).start()
    ld_eig.wait()

    cols = eig_v.shape[1]
    width = 256
    shards = cols // width
    for step, d in enumerate([0] + hops):
        c = lax.rem(col + n_col - d, n_col)
        if d:
            pltpu.make_async_copy(gath.at[c], gath.at[c], z_recv.at[c]).wait()
        base = pl.multiple_of(c * piece, 64)
        lhs_a = jnp.concatenate([gath[c, 0:st, :], gath[c, st : 2 * st, :]], axis=1)
        tail = gath[c, 2 * st : 2 * st + half, :]
        lhs_b = jnp.concatenate([tail[:, 0:64], tail[:, 64:128]], axis=0)
        for n in range(shards):
            span = slice(n * width, (n + 1) * width)
            part = jnp.dot(lhs_a, eig_v[pl.ds(base, 256), span], preferred_element_type=f32)
            part += jnp.dot(lhs_b, eig_v[pl.ds(base + 256, 64), span], preferred_element_type=f32)
            if step:
                part += acc[:, span]
            acc[:, span] = part
            if step == n_col - 1:

                def send_shard(i, carry, n=n):
                    group = lax.rem(row // shards + i, n_row // shards)
                    to = group * shards + n

                    @pl.when(to != row)
                    def _():
                        pltpu.make_async_remote_copy(
                            src_ref=acc.at[pl.ds(pl.multiple_of(group * 8, 8), 8), pl.ds(n * width, width)],
                            dst_ref=rs_recv.at[row],
                            send_sem=rs_send, recv_sem=rs_sem,
                            device_id=(to, col), device_id_type=MESH,
                        ).start()

                    return carry

                lax.fori_loop(0, n_row // shards, send_shard, 0)

    mine = (
        pl.ds(pl.multiple_of((row // shards) * 8, 8), 8),
        pl.ds(pl.multiple_of(lax.rem(row, shards) * width, width), width),
    )
    rs_recv[row] = acc[mine]
    pltpu.make_async_copy(rs_recv.at[many], rs_recv.at[many], rs_sem).wait()
    out_ref[mine] = jnp.sum(rs_recv[...], axis=0)

    def send_result(i, carry):
        pltpu.make_async_remote_copy(
            src_ref=out_ref.at[mine], dst_ref=out_ref.at[mine],
            send_sem=ag_send, recv_sem=ag_sem,
            device_id=(lax.rem(row + i, n_row), col), device_id_type=MESH,
        ).start()
        return carry

    lax.fori_loop(1, n_row, send_result, 0)
    others = gath.at[pl.ds(0, n_col - 1)]
    pltpu.make_async_copy(recv.at[many], recv.at[many], a2a_send).wait()
    pltpu.make_async_copy(others, others, z_send).wait()
    pltpu.make_async_copy(rs_recv.at[many], rs_recv.at[many], rs_send).wait()
    pltpu.make_async_copy(rs_recv.at[many], rs_recv.at[many], ag_sem).wait()
    pltpu.make_async_copy(rs_recv.at[many], rs_recv.at[many], ag_send).wait()


def on_device(n_row, n_col, psi, block_len, targets, counts, dipole, eigvec):
    nb, kmax, _, bs = dipole.shape
    st = psi.shape[1]
    rows, cols = eigvec.shape
    piece = nb * n_row
    bf16, f32 = jnp.bfloat16, jnp.float32
    dma = pltpu.SemaphoreType.DMA
    smem = pl.BlockSpec(memory_space=pltpu.SMEM)
    hbm = pl.BlockSpec(memory_space=pl.ANY)
    turned = pl.pallas_call(
        functools.partial(body, n_row, n_col, nb, kmax, bs, st),
        out_shape=jax.ShapeDtypeStruct((st, cols), f32),
        in_specs=[smem] * 3 + [hbm] * 3,
        out_specs=pl.BlockSpec(memory_space=pltpu.VMEM),
        scratch_shapes=[
            pltpu.VMEM((st, nb * bs), bf16),
            pltpu.VMEM((nb + 2 * WB, st, bs), bf16),
            pltpu.VMEM(dipole.shape, bf16),
            pltpu.VMEM((rows, cols), bf16),
            pltpu.VMEM((n_row * PAD, st), f32),
            pltpu.VMEM((n_row, PAD, st), bf16),
            pltpu.VMEM((n_row, PAD, st), bf16),
            pltpu.VMEM((n_col, piece // 2, 128), bf16),
            pltpu.VMEM((st, cols), f32),
            pltpu.VMEM((n_row, 8, 256), f32),
            dma((3,)),
            dma((2,)),
            dma((2,)),
            dma,
            dma,
            dma,
            dma((n_col,)),
            dma,
            dma,
            dma,
            dma,
        ],
        compiler_params=pltpu.CompilerParams(
            collective_id=0, has_side_effects=True, vmem_limit_bytes=56 * 2**20
        ),
    )(block_len, targets.T, counts, psi.T, dipole, eigvec)
    return turned.T


def solution(mesh):
    placed = (
        P("row", None),
        P("row"),
        P("row", None),
        P("row"),
        P("row", None, "col", None),
        P("row", "col"),
    )
    return jax.shard_map(
        functools.partial(on_device, mesh.shape["row"], mesh.shape["col"]),
        mesh=mesh, in_specs=placed, out_specs=P("col", None), check_vma=False,
    )
```

time: 187 us -> 45.8 us (0.24)
  waiting for transfers between devices: 108 us -> 0 us
  blocking collectives: 45.5 us -> 0 us
  Pallas kernels: 0 us -> 44 us
  between operations: 13.5 us -> 0.01 us
  starting transfers between devices: 6.52 us -> 0 us
  matrix products: 4.79 us -> 0 us
  other arithmetic: 4.01 us -> 0 us
  local copies, waits for them, and re-layouts: 4.32 us -> 1.67 us
    psum x1 -> x0, waiting for transfers between devices: 107 us -> none  [on_device(): return lax.psum(partial_sum, 'row')]
    pallas_call x0 -> x1, Pallas kernels: none -> 44 us  [on_device(): pl.pallas_call(functools.partial(body, n_row, n_col, nb, kmax, bs, st), o...]
    all_gather x1 -> x0, blocking collectives: 24.1 us -> none  [on_device(): gathered = lax.all_gather(pieces, 'col', axis=0, tiled=True)]
    all_to_all x1 -> x0, blocking collectives: 21.4 us -> none  [on_device(): lax.all_to_all(gathered, 'row', split_axis=2, concat_axis=1, tiled=True)]
    ppermute x2 -> x0, starting transfers between devices: 6.52 us -> none  [the longest x1 4.59 us: extended_2(): lax.ppermute(tail, axis, [(i, (i + 1) % count) for i in range(ends)])]
    dot_general x2 -> x0, matrix products: 4.79 us -> none  [the longest x1 4.24 us: on_device(): lax.dot_general(eigvec, flat_rows, (((0,), (0,)), ((), ())), preferred_el...]
    lt x3 -> x0, other arithmetic: 2.25 us -> none  [the longest x1 0.79 us: on_device(): row_used = positions[None, :] < block_len[:, None]]
  transfers between devices with their start and end apart: 3 -> 0, of which waited for: 2 -> 0; matrix products, arithmetic and copies ran while one was open for 1% -> 0% of each run, Pallas kernels for 0% -> 0%
where the time goes in v1:
time: 45.8 us; the launch traced here: 45.7 us
  Pallas kernels  44 us (96%)
  local copies, waits for them, and re-layouts  1.67 us (4%)
    pallas_call x1, Pallas kernels, on_device(): pl.pallas_call(functools.partial(body, n_row, n_col, nb, kmax, bs, st), o...  44 us
    unnamed x1, local copies, waits for them, and re-layouts  1.67 us

profile of v1, /device:TPU:1, one launch (start us, length us, event | category | flops | bytes accessed | tf_op | source)
XLA Modules:
  0.0 45.7 jit_solution(7398597385062467871)
XLA Ops:
  0.0 44.0 %shard_map.64 = f32[64,1024]{1,0:T(8,128)} custom-call(s32[10]{0:T(128)} %lens.1, s32[4,10]{1,0:T(4,128)} %bitcast.5, s32[10]{0:T(128)} %counts.1, bf16[64,2560]{1,0:T(8,128)(2,1)} %bitcast.4, bf16[10,4,32,256]{3,2,1,0:T(8,128)(2,1)} %dip_hbm.1, bf16[2560,1024]{1,0:T(8,128)(2,1)} %eig_hbm.1), custom_call_target="tpu_custom_call" | custom-call | tf_op jit(solution)/shard_map/pallas_call | solution.py:203
  44.0 1.7 %copy.8 = f32[1024,64]{0,1:T(8,128)} copy(f32[1024,64]{0,1:T(8,128)} %bitcast.3) | data formatting | bytes 524288

commit v2 on v0

v2 whole, which is shorter than its diff:
```python
import functools

import jax
import jax.numpy as jnp
from jax import lax
from jax.experimental import pallas as pl
from jax.experimental.pallas import tpu as pltpu
from jax.sharding import PartitionSpec as P

WB = 2
MESH = pl.DeviceIdType.MESH
NT = (((1,), (1,)), ((), ()))
TN = (((0,), (0,)), ((), ()))
PAD = 16
HALVES = 2


def body(
    n_row, n_col, nb, kmax, bs, st,
    lens_hbm, targets_hbm, counts_hbm, psi_hbm, dip_hbm, eig_hbm, out_ref,
    lens, targets, counts, psi_v, own, low, high, dip_v, eig_v, eig_p,
    stage, msg, recv, inner, edge, acc, rs_recv,
    ld_sem, halo_send, halo_recv, a2a_send, a2a_recv, z_send, z_recv, ze_send, ze_recv,
    rs_send, rs_sem, ag_send, ag_sem,
):
    row = lax.axis_index("row")
    col = lax.axis_index("col")
    f32, bf16 = jnp.float32, jnp.bfloat16
    n_edge = 2 * WB
    n_inner = nb - n_edge
    piece = nb * n_row
    k_edge = n_edge * n_row
    k_inner = n_inner * n_row
    cols = eig_v.shape[1]
    half = st // HALVES

    loads = [
        pltpu.make_async_copy(src, dst, ld_sem.at[i])
        for i, (src, dst) in enumerate(
            [
                (lens_hbm, lens),
                (targets_hbm, targets),
                (counts_hbm, counts),
                (psi_hbm, psi_v),
                (dip_hbm, dip_v),
                (eig_hbm, eig_v),
            ]
        )
    ]
    for load in loads:
        load.start()

    barrier = pltpu.get_barrier_semaphore()

    def greet_row(i, carry):
        pl.semaphore_signal(
            barrier, inc=1, device_id=(lax.rem(row + i, n_row), col), device_id_type=MESH
        )
        return carry

    def greet_col(i, carry):
        pl.semaphore_signal(
            barrier, inc=1, device_id=(row, lax.rem(col + i, n_col)), device_id_type=MESH
        )
        return carry

    lax.fori_loop(1, n_row, greet_row, 0)
    lax.fori_loop(1, n_col, greet_col, 0)

    stage[...] = jnp.zeros_like(stage)
    for load in loads[:4]:
        load.wait()

    lane = lax.broadcasted_iota(jnp.int32, (st, bs), 1)
    for b in range(nb):
        block = jnp.where(
            lane < lens[b], psi_v[:, b * bs : (b + 1) * bs], jnp.zeros((), bf16)
        )
        own[b] = block
        if b < 2 * WB:
            low[WB + b] = block
        if b >= nb - 2 * WB:
            high[b - (nb - 2 * WB)] = block
    loads[4].wait()

    kept = lax.broadcasted_iota(jnp.int32, (n_row, st), 0) + col * n_row

    def product(b, blocks, base, at, part):
        top = blocks.shape[0] - 1
        total = jnp.zeros((n_row, st), f32)
        for k in range(kmax):
            chosen = blocks[jnp.clip(targets[k, b] - (row * nb + base), 0, top)]
            chosen = jnp.where(k < counts[b], chosen, jnp.zeros((), bf16))
            total += lax.dot_general(dip_v[b, k], chosen, NT, preferred_element_type=f32)
        total = jnp.where(kept < lens[b], total, 0.0)
        stage[part, pl.ds(at, n_row, stride=PAD), :] = total

    def send_pieces(part):
        msg[part] = stage[part].astype(bf16).reshape(n_row, PAD, st)

        def send(i, carry):
            to = lax.rem(row + i, n_row)
            pltpu.make_async_remote_copy(
                src_ref=msg.at[part, to], dst_ref=recv.at[part, row],
                send_sem=a2a_send.at[part], recv_sem=a2a_recv.at[part],
                device_id=(to, col), device_id_type=MESH,
            ).start()
            return carry

        lax.fori_loop(1, n_row, send, 0)
        recv[part, row] = msg[part, row]

    many = pl.ds(0, n_row - 1)

    def collect(part, count):
        pltpu.make_async_copy(
            recv.at[part, many], recv.at[part, many], a2a_recv.at[part]
        ).wait()
        shape = (n_row * PAD, count * n_row)
        wanted = lax.broadcasted_iota(jnp.int32, shape, 1)
        wanted = wanted + (PAD - count) * (wanted // count)
        select = jnp.where(lax.broadcasted_iota(jnp.int32, shape, 0) == wanted, 1.0, 0.0)
        rows = recv[part].reshape(n_row * PAD, st)
        return lax.dot_general(
            rows, select.astype(bf16), TN, preferred_element_type=f32
        ).astype(bf16)

    for at in range(n_inner):
        product(WB + at, own, 0, at, 0)

    pl.semaphore_wait(barrier, n_row - 1 + n_col - 1)

    to_right = pltpu.make_async_remote_copy(
        src_ref=own.at[pl.ds(nb - WB, WB)], dst_ref=low.at[pl.ds(0, WB)],
        send_sem=halo_send.at[0], recv_sem=halo_recv.at[0],
        device_id=(lax.rem(row + 1, n_row), col), device_id_type=MESH,
    )
    to_left = pltpu.make_async_remote_copy(
        src_ref=own.at[pl.ds(0, WB)], dst_ref=high.at[pl.ds(2 * WB, WB)],
        send_sem=halo_send.at[1], recv_sem=halo_recv.at[1],
        device_id=(lax.rem(row + n_row - 1, n_row), col), device_id_type=MESH,
    )
    to_right.start()
    to_left.start()
    send_pieces(0)

    loads[5].wait()
    place = lax.broadcasted_iota(jnp.int32, (piece, piece), 0)
    group, at = place // n_edge, place % n_edge
    from_edge = group * nb + at + jnp.where(at >= WB, n_inner, 0)
    inner_place = place - k_edge
    from_inner = (inner_place // n_inner) * nb + WB + inner_place % n_inner
    source = jnp.where(place < k_edge, from_edge, from_inner)
    permute = jnp.where(
        lax.broadcasted_iota(jnp.int32, (piece, piece), 1) == source, 1.0, 0.0
    ).astype(bf16)
    for c in range(n_col):
        span = slice(c * piece, (c + 1) * piece)
        eig_p[span, :] = jnp.dot(
            permute, eig_v[span, :], preferred_element_type=f32
        ).astype(bf16)

    to_right.wait()
    to_left.wait()
    for at in range(WB):
        product(at, low, -WB, at, 1)
    for at in range(WB):
        product(nb - WB + at, high, nb - 2 * WB, WB + at, 1)
    send_pieces(1)

    hops = [(s + 1) // 2 if s % 2 else n_col - s // 2 for s in range(1, n_col)]
    turned = collect(0, n_inner)
    inner[col, 0:st, :] = turned[:, 0:128]
    inner[col, st : st + st // 2, :] = jnp.concatenate(
        [turned[: st // 2, 128:k_inner], turned[st // 2 :, 128:k_inner]], axis=1
    )
    for d in hops:
        pltpu.make_async_remote_copy(
            src_ref=inner.at[col], dst_ref=inner.at[col],
            send_sem=z_send, recv_sem=z_recv.at[col],
            device_id=(row, lax.rem(col + d, n_col)), device_id_type=MESH,
        ).start()

    turned = collect(1, n_edge)
    for h in range(HALVES):
        edge[h, col] = turned[h * half : (h + 1) * half, :]
        for d in hops:
            pltpu.make_async_remote_copy(
                src_ref=edge.at[h, col], dst_ref=edge.at[h, col],
                send_sem=ze_send.at[h], recv_sem=ze_recv.at[h, col],
                device_id=(row, lax.rem(col + d, n_col)), device_id_type=MESH,
            ).start()

    for d in [0] + hops:
        c = lax.rem(col + n_col - d, n_col)
        if d:
            pltpu.make_async_copy(inner.at[c], inner.at[c], z_recv.at[c]).wait()
        tail = inner[c, st : st + st // 2, :]
        tail = jnp.concatenate([tail[:, 0:64], tail[:, 64:128]], axis=0)
        lhs = jnp.concatenate([inner[c, 0:st, :], tail], axis=1)
        base = pl.multiple_of(c * piece + k_edge, 64)
        part = jnp.dot(lhs, eig_p[pl.ds(base, k_inner), :], preferred_element_type=f32)
        acc[...] = acc[...] + part if d else part

    lanes = cols // 128
    tile = (
        pl.ds(pl.multiple_of((row // lanes) * 8, 8), 8),
        pl.ds(pl.multiple_of(lax.rem(row, lanes) * 128, 128), 128),
    )
    for h in range(HALVES):
        low_row = h * half
        for d in [0] + hops:
            c = lax.rem(col + n_col - d, n_col)
            if d:
                pltpu.make_async_copy(edge.at[h, c], edge.at[h, c], ze_recv.at[h, c]).wait()
            base = pl.multiple_of(c * piece, 64)
            acc[low_row : low_row + half, :] += jnp.dot(
                edge[h, c], eig_p[pl.ds(base, k_edge), :], preferred_element_type=f32
            )

        def send_tile(i, carry, h=h, low_row=low_row):
            to = lax.rem(row + i, n_row)
            at_row = pl.multiple_of(low_row + (to // lanes) * 8, 8)
            at_lane = pl.multiple_of(lax.rem(to, lanes) * 128, 128)
            pltpu.make_async_remote_copy(
                src_ref=acc.at[pl.ds(at_row, 8), pl.ds(at_lane, 128)],
                dst_ref=rs_recv.at[h, row],
                send_sem=rs_send.at[h], recv_sem=rs_sem.at[h],
                device_id=(to, col), device_id_type=MESH,
            ).start()
            return carry

        lax.fori_loop(1, n_row, send_tile, 0)
        rs_recv[h, row] = acc[
            pl.ds(pl.multiple_of(low_row + (row // lanes) * 8, 8), 8), tile[1]
        ]

    for h in range(HALVES):
        pltpu.make_async_copy(
            rs_recv.at[h, many], rs_recv.at[h, many], rs_sem.at[h]
        ).wait()
        mine = (pl.ds(pl.multiple_of(h * half + (row // lanes) * 8, 8), 8), tile[1])
        out_ref[mine] = jnp.sum(rs_recv[h], axis=0)

        def send_result(i, carry, h=h, mine=mine):
            pltpu.make_async_remote_copy(
                src_ref=out_ref.at[mine], dst_ref=out_ref.at[mine],
                send_sem=ag_send.at[h], recv_sem=ag_sem.at[h],
                device_id=(lax.rem(row + i, n_row), col), device_id_type=MESH,
            ).start()
            return carry

        lax.fori_loop(1, n_row, send_result, 0)

    others = pl.ds(0, n_col - 1)
    pltpu.make_async_copy(inner.at[others], inner.at[others], z_send).wait()
    for h in range(HALVES):
        pltpu.make_async_copy(recv.at[h, many], recv.at[h, many], a2a_send.at[h]).wait()
        pltpu.make_async_copy(edge.at[h, others], edge.at[h, others], ze_send.at[h]).wait()
        pltpu.make_async_copy(rs_recv.at[h, many], rs_recv.at[h, many], rs_send.at[h]).wait()
    for h in range(HALVES):
        pltpu.make_async_copy(rs_recv.at[h, many], rs_recv.at[h, many], ag_sem.at[h]).wait()
        pltpu.make_async_copy(rs_recv.at[h, many], rs_recv.at[h, many], ag_send.at[h]).wait()


def on_device(n_row, n_col, psi, block_len, targets, counts, dipole, eigvec):
    nb, kmax, _, bs = dipole.shape
    st = psi.shape[1]
    rows, cols = eigvec.shape
    n_edge, n_inner = 2 * WB, nb - 2 * WB
    bf16, f32, i32 = jnp.bfloat16, jnp.float32, jnp.int32
    dma = pltpu.SemaphoreType.DMA
    operands = [
        pltpu.with_memory_space_constraint(a, pltpu.HBM)
        for a in (block_len, targets.T, counts, psi.T, dipole, eigvec)
    ]
    turned = pl.pallas_call(
        functools.partial(body, n_row, n_col, nb, kmax, bs, st),
        out_shape=jax.ShapeDtypeStruct((st, cols), f32),
        in_specs=[pl.BlockSpec(memory_space=pltpu.HBM)] * 6,
        out_specs=pl.BlockSpec(memory_space=pltpu.VMEM),
        scratch_shapes=[
            pltpu.SMEM((nb,), i32),
            pltpu.SMEM((kmax, nb), i32),
            pltpu.SMEM((nb,), i32),
            pltpu.VMEM((st, nb * bs), bf16),
            pltpu.VMEM((nb, st, bs), bf16),
            pltpu.VMEM((3 * WB, st, bs), bf16),
            pltpu.VMEM((3 * WB, st, bs), bf16),
            pltpu.VMEM(dipole.shape, bf16),
            pltpu.VMEM((rows, cols), bf16),
            pltpu.VMEM((rows, cols), bf16),
            pltpu.VMEM((2, n_row * PAD, st), f32),
            pltpu.VMEM((2, n_row, PAD, st), bf16),
            pltpu.VMEM((2, n_row, PAD, st), bf16),
            pltpu.VMEM((n_col, n_inner * n_row // 2, 128), bf16),
            pltpu.VMEM((HALVES, n_col, st // HALVES, n_edge * n_row), bf16),
            pltpu.VMEM((st, cols), f32),
            pltpu.VMEM((HALVES, n_row, 8, 128), f32),
            dma((6,)),
            dma((2,)),
            dma((2,)),
            dma((2,)),
            dma((2,)),
            dma,
            dma((n_col,)),
            dma((HALVES,)),
            dma((HALVES, n_col)),
            dma((HALVES,)),
            dma((HALVES,)),
            dma((HALVES,)),
            dma((HALVES,)),
        ],
        compiler_params=pltpu.CompilerParams(
            collective_id=0, has_side_effects=True, vmem_limit_bytes=24 * 2**20
        ),
    )(*operands)
    return turned.T


def solution(mesh):
    placed = (
        P("row", None),
        P("row"),
        P("row", None),
        P("row"),
        P("row", None, "col", None),
        P("row", "col"),
    )
    return jax.shard_map(
        functools.partial(on_device, mesh.shape["row"], mesh.shape["col"]),
        mesh=mesh, in_specs=placed, out_specs=P("col", None), check_vma=False,
    )
```

time: 187 us -> 39.8 us (0.21)
  waiting for transfers between devices: 108 us -> 0 us
  blocking collectives: 45.5 us -> 0 us
  Pallas kernels: 0 us -> 39.1 us
  between operations: 13.5 us -> 0.01 us
  starting transfers between devices: 6.52 us -> 0 us
  matrix products: 4.79 us -> 0 us
  other arithmetic: 4.01 us -> 0 us
  local copies, waits for them, and re-layouts: 4.32 us -> 0.71 us
    psum x1 -> x0, waiting for transfers between devices: 107 us -> none  [on_device(): return lax.psum(partial_sum, 'row')]
    pallas_call x0 -> x1, Pallas kernels: none -> 39.1 us  [on_device(): pl.pallas_call(functools.partial(body, n_row, n_col, nb, kmax, bs, st), o...]
    all_gather x1 -> x0, blocking collectives: 24.1 us -> none  [on_device(): gathered = lax.all_gather(pieces, 'col', axis=0, tiled=True)]
    all_to_all x1 -> x0, blocking collectives: 21.4 us -> none  [on_device(): lax.all_to_all(gathered, 'row', split_axis=2, concat_axis=1, tiled=True)]
    ppermute x2 -> x0, starting transfers between devices: 6.52 us -> none  [the longest x1 4.59 us: extended_2(): lax.ppermute(tail, axis, [(i, (i + 1) % count) for i in range(ends)])]
    dot_general x2 -> x0, matrix products: 4.79 us -> none  [the longest x1 4.24 us: on_device(): lax.dot_general(eigvec, flat_rows, (((0,), (0,)), ((), ())), preferred_el...]
    lt x3 -> x0, other arithmetic: 2.25 us -> none  [the longest x1 0.79 us: on_device(): row_used = positions[None, :] < block_len[:, None]]
  transfers between devices with their start and end apart: 3 -> 0, of which waited for: 2 -> 0; matrix products, arithmetic and copies ran while one was open for 1% -> 0% of each run, Pallas kernels for 0% -> 0%
where the time goes in v2:
time: 39.8 us
  Pallas kernels  39.1 us (98%)
  local copies, waits for them, and re-layouts  0.71 us (2%)
    pallas_call x1, Pallas kernels, on_device(): pl.pallas_call(functools.partial(body, n_row, n_col, nb, kmax, bs, st), o...  39.1 us

profile of v2, /device:TPU:1, one launch (start us, length us, event | category | flops | bytes accessed | tf_op | source)
XLA Modules:
  0.0 39.8 jit_solution(6618854717619693898)
XLA Ops:
  0.0 39.1 %shard_map.64 = f32[64,1024]{1,0:T(8,128)S(1)} custom-call(s32[10]{0:T(128)} %lens_hbm.1, s32[4,10]{1,0:T(4,128)} %bitcast.5, s32[10]{0:T(128)} %counts_hbm.1, bf16[64,2560]{1,0:T(8,128)(2,1)} %bitcast.4, bf16[10,4,32,256]{3,2,1,0:T(8,128)(2,1)} %dip_hbm.1, bf16[2560,1024]{1,0:T(8,128)(2,1)} %eig_hbm.1), custom_call_target="tpu_custom_call" | custom-call | tf_op jit(solution)/shard_map/pallas_call | solution.py:277
  39.1 0.7 %copy.8 = f32[1024,64]{0,1:T(8,128)} copy(f32[1024,64]{0,1:T(8,128)S(1)} %bitcast.3) | data formatting | bytes 524288

commit v3 on v2

--- a/solution.py
+++ b/solution.py
@@ -11,7 +11,6 @@
 MESH = pl.DeviceIdType.MESH
 NT = (((1,), (1,)), ((), ()))
 TN = (((0,), (0,)), ((), ()))
-PAD = 16
 HALVES = 2
 
 
@@ -19,7 +18,7 @@
     n_row, n_col, nb, kmax, bs, st,
     lens_hbm, targets_hbm, counts_hbm, psi_hbm, dip_hbm, eig_hbm, out_ref,
     lens, targets, counts, psi_v, own, low, high, dip_v, eig_v, eig_p,
-    stage, msg, recv, inner, edge, acc, rs_recv,
+    inner_msg, edge_msg, inner_recv, edge_recv, inner, edge, acc, rs_recv,
     ld_sem, halo_send, halo_recv, a2a_send, a2a_recv, z_send, z_recv, ze_send, ze_recv,
     rs_send, rs_sem, ag_send, ag_sem,
 ):
@@ -47,27 +46,49 @@
             ]
         )
     ]
+
+    chip_x, chip_y, core = row // 8, lax.rem(row // 2, 4), lax.rem(row, 2)
+    at_x = [lax.rem(chip_x + d, 4) for d in range(4)]
+    at_y = [[lax.rem(chip_y + d, 4) * 2 + c for c in (core, 1 - core)] for d in range(4)]
+    offsets = [(x, y, c) for x in range(4) for y in range(4) for c in range(2)][1:]
+    offsets.sort(key=lambda o: -(min(o[0], 4 - o[0]) + min(o[1], 4 - o[1])))
+    peers = [(at_x[x], at_y[y][c]) for x, y, c in offsets]
+
+    barrier = pltpu.get_barrier_semaphore()
+
+    for x, y in peers:
+        pl.semaphore_signal(
+            barrier, inc=1, device_id=(x * 8 + y, col), device_id_type=MESH
+        )
+    for i in range(1, n_col):
+        pl.semaphore_signal(
+            barrier, inc=1, device_id=(row, lax.rem(col + i, n_col)), device_id_type=MESH
+        )
     for load in loads:
         load.start()
 
-    barrier = pltpu.get_barrier_semaphore()
-
-    def greet_row(i, carry):
-        pl.semaphore_signal(
-            barrier, inc=1, device_id=(lax.rem(row + i, n_row), col), device_id_type=MESH
-        )
-        return carry
-
-    def greet_col(i, carry):
-        pl.semaphore_signal(
-            barrier, inc=1, device_id=(row, lax.rem(col + i, n_col)), device_id_type=MESH
-        )
-        return carry
-
-    lax.fori_loop(1, n_row, greet_row, 0)
-    lax.fori_loop(1, n_col, greet_col, 0)
-
-    stage[...] = jnp.zeros_like(stage)
+    def rows_are(count, wanted):
+        held = lax.broadcasted_iota(jnp.int32, (count, wanted.shape[1]), 0)
+        return jnp.where(held == wanted, 1.0, 0.0).astype(bf16)
+
+    def kept_rows(used, held):
+        at = lax.broadcasted_iota(jnp.int32, (1, used * n_row), 1)
+        return rows_are(held * n_row, at + (held - used) * (at // used))
+
+    select_inner = kept_rows(n_inner // 2, inner_msg.shape[1])
+    select_edge = kept_rows(WB, edge_msg.shape[1])
+    at = lax.broadcasted_iota(jnp.int32, (1, piece), 1)
+    group, at = at // nb, at % nb
+    late = at >= nb - WB
+    at_edge = jnp.where(late, at - (nb - WB), at)
+    to_edge = at_edge * (k_edge // 2) + group * 2 + jnp.where(late, 1, 0)
+    at_inner = at - WB
+    third = n_inner // 2
+    to_inner = (at_inner // third) * (k_inner // 2) + group * third + at_inner % third
+    permute = rows_are(piece, jnp.where((at < WB) | late, to_edge, k_edge + to_inner))
+
+    for r in range(third, inner_msg.shape[1]):
+        inner_msg[:, r, :] = jnp.zeros((n_row, 128), f32)
     for load in loads[:4]:
         load.wait()
 
@@ -85,48 +106,37 @@
 
     kept = lax.broadcasted_iota(jnp.int32, (n_row, st), 0) + col * n_row
 
-    def product(b, blocks, base, at, part):
+    def product(b, blocks, base):
         top = blocks.shape[0] - 1
         total = jnp.zeros((n_row, st), f32)
         for k in range(kmax):
             chosen = blocks[jnp.clip(targets[k, b] - (row * nb + base), 0, top)]
             chosen = jnp.where(k < counts[b], chosen, jnp.zeros((), bf16))
             total += lax.dot_general(dip_v[b, k], chosen, NT, preferred_element_type=f32)
-        total = jnp.where(kept < lens[b], total, 0.0)
-        stage[part, pl.ds(at, n_row, stride=PAD), :] = total
-
-    def send_pieces(part):
-        msg[part] = stage[part].astype(bf16).reshape(n_row, PAD, st)
-
-        def send(i, carry):
-            to = lax.rem(row + i, n_row)
+        return jnp.where(kept < lens[b], total, 0.0).astype(bf16).astype(f32)
+
+    def send_pieces(part, msg, recv):
+        for x, y in peers:
+            to = x * 8 + y
             pltpu.make_async_remote_copy(
-                src_ref=msg.at[part, to], dst_ref=recv.at[part, row],
+                src_ref=msg.at[to], dst_ref=recv.at[row],
                 send_sem=a2a_send.at[part], recv_sem=a2a_recv.at[part],
                 device_id=(to, col), device_id_type=MESH,
             ).start()
-            return carry
-
-        lax.fori_loop(1, n_row, send, 0)
-        recv[part, row] = msg[part, row]
+        recv[row] = msg[row]
 
     many = pl.ds(0, n_row - 1)
 
-    def collect(part, count):
-        pltpu.make_async_copy(
-            recv.at[part, many], recv.at[part, many], a2a_recv.at[part]
-        ).wait()
-        shape = (n_row * PAD, count * n_row)
-        wanted = lax.broadcasted_iota(jnp.int32, shape, 1)
-        wanted = wanted + (PAD - count) * (wanted // count)
-        select = jnp.where(lax.broadcasted_iota(jnp.int32, shape, 0) == wanted, 1.0, 0.0)
-        rows = recv[part].reshape(n_row * PAD, st)
-        return lax.dot_general(
-            rows, select.astype(bf16), TN, preferred_element_type=f32
-        ).astype(bf16)
-
-    for at in range(n_inner):
-        product(WB + at, own, 0, at, 0)
+    def collect(part, recv, select):
+        pltpu.make_async_copy(recv.at[many], recv.at[many], a2a_recv.at[part]).wait()
+        rows = recv[...].reshape(-1, 128).astype(bf16)
+        both = lax.dot_general(rows, select, TN, preferred_element_type=f32).astype(bf16)
+        return jnp.concatenate([both[:st], both[st:]], axis=1)
+
+    for r in range(third):
+        inner_msg[:, r, :] = jnp.concatenate(
+            [product(WB + r, own, 0), product(WB + third + r, own, 0)], axis=1
+        )
 
     pl.semaphore_wait(barrier, n_row - 1 + n_col - 1)
 
@@ -142,18 +152,9 @@
     )
     to_right.start()
     to_left.start()
-    send_pieces(0)
+    send_pieces(0, inner_msg, inner_recv)
 
     loads[5].wait()
-    place = lax.broadcasted_iota(jnp.int32, (piece, piece), 0)
-    group, at = place // n_edge, place % n_edge
-    from_edge = group * nb + at + jnp.where(at >= WB, n_inner, 0)
-    inner_place = place - k_edge
-    from_inner = (inner_place // n_inner) * nb + WB + inner_place % n_inner
-    source = jnp.where(place < k_edge, from_edge, from_inner)
-    permute = jnp.where(
-        lax.broadcasted_iota(jnp.int32, (piece, piece), 1) == source, 1.0, 0.0
-    ).astype(bf16)
     for c in range(n_col):
         span = slice(c * piece, (c + 1) * piece)
         eig_p[span, :] = jnp.dot(
@@ -162,29 +163,30 @@
 
     to_right.wait()
     to_left.wait()
-    for at in range(WB):
-        product(at, low, -WB, at, 1)
-    for at in range(WB):
-        product(nb - WB + at, high, nb - 2 * WB, WB + at, 1)
-    send_pieces(1)
+    edge_msg[:, 0, :] = jnp.concatenate([product(b, low, -WB) for b in range(WB)], axis=1)
+    edge_msg[:, 1, :] = jnp.concatenate(
+        [product(b, high, nb - 2 * WB) for b in range(nb - WB, nb)], axis=1
+    )
+    send_pieces(1, edge_msg, edge_recv)
 
     hops = [(s + 1) // 2 if s % 2 else n_col - s // 2 for s in range(1, n_col)]
-    turned = collect(0, n_inner)
+    far_first = hops[::-1]
+    turned = collect(0, inner_recv, select_inner)
     inner[col, 0:st, :] = turned[:, 0:128]
     inner[col, st : st + st // 2, :] = jnp.concatenate(
         [turned[: st // 2, 128:k_inner], turned[st // 2 :, 128:k_inner]], axis=1
     )
-    for d in hops:
+    for d in far_first:
         pltpu.make_async_remote_copy(
             src_ref=inner.at[col], dst_ref=inner.at[col],
             send_sem=z_send, recv_sem=z_recv.at[col],
             device_id=(row, lax.rem(col + d, n_col)), device_id_type=MESH,
         ).start()
 
-    turned = collect(1, n_edge)
+    turned = collect(1, edge_recv, select_edge)
     for h in range(HALVES):
         edge[h, col] = turned[h * half : (h + 1) * half, :]
-        for d in hops:
+        for d in far_first:
             pltpu.make_async_remote_copy(
                 src_ref=edge.at[h, col], dst_ref=edge.at[h, col],
                 send_sem=ze_send.at[h], recv_sem=ze_recv.at[h, col],
@@ -218,19 +220,15 @@
                 edge[h, c], eig_p[pl.ds(base, k_edge), :], preferred_element_type=f32
             )
 
-        def send_tile(i, carry, h=h, low_row=low_row):
-            to = lax.rem(row + i, n_row)
-            at_row = pl.multiple_of(low_row + (to // lanes) * 8, 8)
-            at_lane = pl.multiple_of(lax.rem(to, lanes) * 128, 128)
+        for x, y in peers:
+            at_row = pl.multiple_of(low_row + x * 8, 8)
+            at_lane = pl.multiple_of(y * 128, 128)
             pltpu.make_async_remote_copy(
                 src_ref=acc.at[pl.ds(at_row, 8), pl.ds(at_lane, 128)],
                 dst_ref=rs_recv.at[h, row],
                 send_sem=rs_send.at[h], recv_sem=rs_sem.at[h],
-                device_id=(to, col), device_id_type=MESH,
+                device_id=(x * 8 + y, col), device_id_type=MESH,
             ).start()
-            return carry
-
-        lax.fori_loop(1, n_row, send_tile, 0)
         rs_recv[h, row] = acc[
             pl.ds(pl.multiple_of(low_row + (row // lanes) * 8, 8), 8), tile[1]
         ]
@@ -242,20 +240,18 @@
         mine = (pl.ds(pl.multiple_of(h * half + (row // lanes) * 8, 8), 8), tile[1])
         out_ref[mine] = jnp.sum(rs_recv[h], axis=0)
 
-        def send_result(i, carry, h=h, mine=mine):
+        for x, y in peers:
             pltpu.make_async_remote_copy(
                 src_ref=out_ref.at[mine], dst_ref=out_ref.at[mine],
                 send_sem=ag_send.at[h], recv_sem=ag_sem.at[h],
-                device_id=(lax.rem(row + i, n_row), col), device_id_type=MESH,
+                device_id=(x * 8 + y, col), device_id_type=MESH,
             ).start()
-            return carry
-
-        lax.fori_loop(1, n_row, send_result, 0)
 
     others = pl.ds(0, n_col - 1)
     pltpu.make_async_copy(inner.at[others], inner.at[others], z_send).wait()
     for h in range(HALVES):
-        pltpu.make_async_copy(recv.at[h, many], recv.at[h, many], a2a_send.at[h]).wait()
+        sent = (inner_msg, edge_msg)[h].at[many]
+        pltpu.make_async_copy(sent, sent, a2a_send.at[h]).wait()
         pltpu.make_async_copy(edge.at[h, others], edge.at[h, others], ze_send.at[h]).wait()
         pltpu.make_async_copy(rs_recv.at[h, many], rs_recv.at[h, many], rs_send.at[h]).wait()
     for h in range(HALVES):
@@ -290,9 +286,10 @@
             pltpu.VMEM(dipole.shape, bf16),
             pltpu.VMEM((rows, cols), bf16),
             pltpu.VMEM((rows, cols), bf16),
-            pltpu.VMEM((2, n_row * PAD, st), f32),
-            pltpu.VMEM((2, n_row, PAD, st), bf16),
-            pltpu.VMEM((2, n_row, PAD, st), bf16),
+            pltpu.VMEM((n_row, 4, 128), f32),
+            pltpu.VMEM((n_row, 2, 128), f32),
+            pltpu.VMEM((n_row, 4, 128), f32),
+            pltpu.VMEM((n_row, 2, 128), f32),
             pltpu.VMEM((n_col, n_inner * n_row // 2, 128), bf16),
             pltpu.VMEM((HALVES, n_col, st // HALVES, n_edge * n_row), bf16),
             pltpu.VMEM((st, cols), f32),

time: 39.8 us -> 37.5 us (0.942)
  Pallas kernels: 39.1 us -> 36.7 us
    pallas_call x1, Pallas kernels: 39.1 us -> 36.7 us  [on_device(): pl.pallas_call(functools.partial(body, n_row, n_col, nb, kmax, bs, st), o...]
where the time goes in v3:
time: 37.5 us; the launch traced here: 37.4 us
  Pallas kernels  36.7 us (98%)
  local copies, waits for them, and re-layouts  0.71 us (2%)
    pallas_call x1, Pallas kernels, on_device(): pl.pallas_call(functools.partial(body, n_row, n_col, nb, kmax, bs, st), o...  36.7 us

profile of v3, /device:TPU:1, one launch (start us, length us, event | category | flops | bytes accessed | tf_op | source)
XLA Modules:
  0.0 37.4 jit_solution(2740849998194611181)
XLA Ops:
  0.0 36.7 %shard_map.64 = f32[64,1024]{1,0:T(8,128)S(1)} custom-call(s32[10]{0:T(128)} %lens_hbm.1, s32[4,10]{1,0:T(4,128)} %bitcast.5, s32[10]{0:T(128)} %counts_hbm.1, bf16[64,2560]{1,0:T(8,128)(2,1)} %bitcast.4, bf16[10,4,32,256]{3,2,1,0:T(8,128)(2,1)} %dip_hbm.1, bf16[2560,1024]{1,0:T(8,128)(2,1)} %eig_hbm.1), custom_call_target="tpu_custom_call" | custom-call | tf_op jit(solution)/shard_map/pallas_call | solution.py:273
  36.7 0.7 %copy.8 = f32[1024,64]{0,1:T(8,128)} copy(f32[1024,64]{0,1:T(8,128)S(1)} %bitcast.3) | data formatting | bytes 524288

commit v4 on v3

--- a/solution.py
+++ b/solution.py
@@ -76,7 +76,6 @@
         return rows_are(held * n_row, at + (held - used) * (at // used))
 
     select_inner = kept_rows(n_inner // 2, inner_msg.shape[1])
-    select_edge = kept_rows(WB, edge_msg.shape[1])
     at = lax.broadcasted_iota(jnp.int32, (1, piece), 1)
     group, at = at // nb, at % nb
     late = at >= nb - WB
@@ -108,11 +107,19 @@
 
     def product(b, blocks, base):
         top = blocks.shape[0] - 1
-        total = jnp.zeros((n_row, st), f32)
-        for k in range(kmax):
-            chosen = blocks[jnp.clip(targets[k, b] - (row * nb + base), 0, top)]
-            chosen = jnp.where(k < counts[b], chosen, jnp.zeros((), bf16))
-            total += lax.dot_general(dip_v[b, k], chosen, NT, preferred_element_type=f32)
+        chosen = [
+            jnp.where(
+                k < counts[b],
+                blocks[jnp.clip(targets[k, b] - (row * nb + base), 0, top)],
+                jnp.zeros((), bf16),
+            )
+            for k in range(kmax)
+        ]
+        total = lax.dot_general(
+            jnp.concatenate([dip_v[b, k] for k in range(kmax)], axis=1),
+            jnp.concatenate(chosen, axis=1),
+            NT, preferred_element_type=f32,
+        )
         return jnp.where(kept < lens[b], total, 0.0).astype(bf16).astype(f32)
 
     def send_pieces(part, msg, recv):
@@ -129,8 +136,13 @@
 
     def collect(part, recv, select):
         pltpu.make_async_copy(recv.at[many], recv.at[many], a2a_recv.at[part]).wait()
-        rows = recv[...].reshape(-1, 128).astype(bf16)
-        both = lax.dot_general(rows, select, TN, preferred_element_type=f32).astype(bf16)
+        rows = recv[...].reshape(-1, 128)
+        if select is None:
+            both = rows.T.astype(bf16)
+        else:
+            both = lax.dot_general(
+                rows.astype(bf16), select, TN, preferred_element_type=f32
+            ).astype(bf16)
         return jnp.concatenate([both[:st], both[st:]], axis=1)
 
     for r in range(third):
@@ -150,9 +162,9 @@
         send_sem=halo_send.at[1], recv_sem=halo_recv.at[1],
         device_id=(lax.rem(row + n_row - 1, n_row), col), device_id_type=MESH,
     )
+    send_pieces(0, inner_msg, inner_recv)
     to_right.start()
     to_left.start()
-    send_pieces(0, inner_msg, inner_recv)
 
     loads[5].wait()
     for c in range(n_col):
@@ -161,8 +173,8 @@
             permute, eig_v[span, :], preferred_element_type=f32
         ).astype(bf16)
 
-    to_right.wait()
-    to_left.wait()
+    to_right.wait_recv()
+    to_left.wait_recv()
     edge_msg[:, 0, :] = jnp.concatenate([product(b, low, -WB) for b in range(WB)], axis=1)
     edge_msg[:, 1, :] = jnp.concatenate(
         [product(b, high, nb - 2 * WB) for b in range(nb - WB, nb)], axis=1
@@ -183,7 +195,7 @@
             device_id=(row, lax.rem(col + d, n_col)), device_id_type=MESH,
         ).start()
 
-    turned = collect(1, edge_recv, select_edge)
+    turned = collect(1, edge_recv, None)
     for h in range(HALVES):
         edge[h, col] = turned[h * half : (h + 1) * half, :]
         for d in far_first:
@@ -247,6 +259,8 @@
                 device_id=(x * 8 + y, col), device_id_type=MESH,
             ).start()
 
+    to_right.wait_send()
+    to_left.wait_send()
     others = pl.ds(0, n_col - 1)
     pltpu.make_async_copy(inner.at[others], inner.at[others], z_send).wait()
     for h in range(HALVES):

time: 37.5 us -> 37.3 us (level)
  no operation moved by 1% of the time
where the time goes in v4:
time: 37.3 us; the launch traced here: 37.2 us
  Pallas kernels  36.5 us (98%)
  local copies, waits for them, and re-layouts  0.71 us (2%)
    pallas_call x1, Pallas kernels, on_device(): pl.pallas_call(functools.partial(body, n_row, n_col, nb, kmax, bs, st), o...  36.5 us

profile of v4, /device:TPU:1, one launch (start us, length us, event | category | flops | bytes accessed | tf_op | source)
XLA Modules:
  0.0 37.2 jit_solution(9386821743148934912)
XLA Ops:
  0.0 36.5 %shard_map.64 = f32[64,1024]{1,0:T(8,128)S(1)} custom-call(s32[10]{0:T(128)} %lens_hbm.1, s32[4,10]{1,0:T(4,128)} %bitcast.5, s32[10]{0:T(128)} %counts_hbm.1, bf16[64,2560]{1,0:T(8,128)(2,1)} %bitcast.4, bf16[10,4,32,256]{3,2,1,0:T(8,128)(2,1)} %dip_hbm.1, bf16[2560,1024]{1,0:T(8,128)(2,1)} %eig_hbm.1), custom_call_target="tpu_custom_call" | custom-call | tf_op jit(solution)/shard_map/pallas_call | solution.py:287
  36.5 0.7 %copy.8 = f32[1024,64]{0,1:T(8,128)} copy(f32[1024,64]{0,1:T(8,128)S(1)} %bitcast.3) | data formatting | bytes 524288

commit v5 on v4

--- a/solution.py
+++ b/solution.py
@@ -51,7 +51,7 @@
     at_x = [lax.rem(chip_x + d, 4) for d in range(4)]
     at_y = [[lax.rem(chip_y + d, 4) * 2 + c for c in (core, 1 - core)] for d in range(4)]
     offsets = [(x, y, c) for x in range(4) for y in range(4) for c in range(2)][1:]
-    offsets.sort(key=lambda o: -(min(o[0], 4 - o[0]) + min(o[1], 4 - o[1])))
+    offsets.sort(key=lambda o: (-(min(o[0], 4 - o[0]) + min(o[1], 4 - o[1])), o[2], (o[0] * 3 + o[1] * 5) % 7))
     peers = [(at_x[x], at_y[y][c]) for x, y, c in offsets]
 
     barrier = pltpu.get_barrier_semaphore()

time: 37.3 us -> 37.3 us (level)
  no operation moved by 1% of the time
where the time goes in v5:
time: 37.3 us; the launch traced here: 37.2 us
  Pallas kernels  36.5 us (98%)
  local copies, waits for them, and re-layouts  0.71 us (2%)
    pallas_call x1, Pallas kernels, on_device(): pl.pallas_call(functools.partial(body, n_row, n_col, nb, kmax, bs, st), o...  36.5 us

profile of v5, /device:TPU:1, one launch (start us, length us, event | category | flops | bytes accessed | tf_op | source)
XLA Modules:
  0.0 37.2 jit_solution(15443942766046711242)
XLA Ops:
  0.0 36.5 %shard_map.64 = f32[64,1024]{1,0:T(8,128)S(1)} custom-call(s32[10]{0:T(128)} %lens_hbm.1, s32[4,10]{1,0:T(4,128)} %bitcast.5, s32[10]{0:T(128)} %counts_hbm.1, bf16[64,2560]{1,0:T(8,128)(2,1)} %bitcast.4, bf16[10,4,32,256]{3,2,1,0:T(8,128)(2,1)} %dip_hbm.1, bf16[2560,1024]{1,0:T(8,128)(2,1)} %eig_hbm.1), custom_call_target="tpu_custom_call" | custom-call | tf_op jit(solution)/shard_map/pallas_call | solution.py:287
  36.5 0.7 %copy.8 = f32[1024,64]{0,1:T(8,128)} copy(f32[1024,64]{0,1:T(8,128)S(1)} %bitcast.3) | data formatting | bytes 524288
